TPU v7x, 256 devices: a whole 4x4x8 slice. The times are simulated.
256 devices in a mesh: section: 2 (over z_lo), dp: 16 (over y, z_hi), tensor: 8 (over x, core).
Axes of the slice: x: 4, y: 4, z: 8 (z_hi: 4, z_lo: 2; z = z_hi * 2 + z_lo), core: 2. Of those that a mesh axis runs over, the one named last changes fastest.
Arguments:
- outgoing: bfloat16 [2, 32768, 8192], P('section', 'dp', 'tensor'), may hold values from -6 to 6
- embedding: bfloat16 [64256, 8192], P(('section', 'dp'), 'tensor'), may hold values from -3 to 3
- shared_basis: bfloat16 [8192, 512], P('tensor'), may hold values from -0.0625 to 0.0625
- token_ids: int32 [2, 32768], P('section', 'dp'), may hold values from 0 to 64255, as said below
- row_route: int32 [2, 32768], P('section', 'dp'), may hold values from 0 to 32767, as said below
Outputs:
- lifted: bfloat16 [2, 32768, 8192], P('section', 'dp', 'tensor')
Inputs may be any that keep to these rules, and one draw needn't show every extreme that they name: row_route[0] is a permutation of the 32768 rows and row_route[1] is its inverse; the 2048 rows of one dp index in one section go to exactly 2048 / 16 rows of each dp index in the other section. token_ids[1, row_route[0, r]] = token_ids[0, r]; the 2048 rows of one dp index in either section name each of the 32 aligned vocabulary blocks of 2008 ids exactly 2048 / 32 times.
All inputs are finite; a program needn't handle non-finite values.
Results may differ from a plain program's by a relative error of at most 0.0044.
Values may be sent and summed in bfloat16 or wider, within the bound.
A program may use at most 64 MiB of HBM per device.

v0:
```python
import jax
import jax.numpy as jnp
from jax import lax
from jax.sharding import PartitionSpec as P


def from_partner(value, axis, stride):
    mask = 2**stride
    pairs = [(source, source ^ mask) for source in range(lax.axis_size(axis))]
    return lax.ppermute(value, axis, pairs)


def on_device(outgoing, embedding, shared_basis, token_ids, row_route):
    section_index = lax.axis_index("section")
    forward_flag = (section_index == 0).astype(jnp.float32)
    own_ids = token_ids[0]
    own_route = row_route[0]
    own_acts = outgoing[0]
    tok_count = own_ids.shape[0]
    owner_count = lax.axis_size(("section", "dp"))
    per_owner = tok_count // owner_count
    vocab_block = embedding.shape[0]
    positions = jnp.arange(tok_count, dtype=jnp.int32)
    owner_of = own_ids // vocab_block
    ask_order = jnp.argsort(owner_of * tok_count + positions)
    asked_ids = own_ids[ask_order].reshape(owner_count, per_owner)
    arrived_ids = lax.all_to_all(
        asked_ids, ("section", "dp"), split_axis=0, concat_axis=0, tiled=True
    )
    local_index = arrived_ids - lax.axis_index(("section", "dp")) * vocab_block
    looked_up = embedding[local_index]
    returned_rows = lax.all_to_all(
        looked_up, ("section", "dp"), split_axis=0, concat_axis=0, tiled=True
    )
    undo_order = jnp.argsort(ask_order)
    embed_rows = returned_rows.reshape(tok_count, -1)[undo_order]
    hidden_rows = (
        own_acts.astype(jnp.float32) - forward_flag * embed_rows.astype(jnp.float32)
    ).astype(jnp.bfloat16)
    dp_count = lax.axis_size("dp")
    tensor_count = lax.axis_size("tensor")
    group_rows = tok_count // dp_count
    piece_count = group_rows // tensor_count
    target_dp = own_route // tok_count
    send_order = jnp.argsort(target_dp * tok_count + positions)
    send_order = (
        send_order.reshape(dp_count, tensor_count, piece_count)
        .transpose(1, 0, 2)
        .reshape(tok_count)
    )
    partial_coef = jnp.dot(hidden_rows, shared_basis, preferred_element_type=jnp.float32)
    ordered_coef = partial_coef[send_order]
    share_rows = tok_count // tensor_count
    summed = lax.psum(ordered_coef, "tensor")
    mine_rows = lax.dynamic_slice_in_dim(
        summed, lax.axis_index("tensor") * share_rows, share_rows, 0
    )
    coef_rows = mine_rows.astype(jnp.bfloat16).reshape(dp_count, piece_count, -1)
    moved_rows = lax.all_to_all(coef_rows, "dp", split_axis=0, concat_axis=0, tiled=True)
    moved_rows = from_partner(moved_rows, "section", 0)
    recv_order = jnp.argsort(own_route)
    recv_rank = jnp.argsort(recv_order)
    fetch_index = (
        recv_rank % group_rows // piece_count * (dp_count * piece_count)
        + recv_rank // group_rows * piece_count
        + recv_rank % piece_count
    )
    all_coef = lax.all_gather(
        moved_rows.reshape(dp_count * piece_count, -1), "tensor", axis=0, tiled=True
    )
    placed_coef = all_coef[fetch_index]
    lifted_rows = lax.dot_general(
        placed_coef, shared_basis, (((1,), (1,)), ((), ())), preferred_element_type=jnp.float32
    )
    result_rows = (lifted_rows + (1.0 - forward_flag) * embed_rows.astype(jnp.float32)).astype(
        jnp.bfloat16
    )
    return result_rows[None]


def solution(mesh):
    return jax.shard_map(
        on_device,
        mesh=mesh,
        in_specs=(
            P("section", "dp", "tensor"),
            P(("section", "dp"), "tensor"),
            P("tensor", None),
            P("section", "dp"),
            P("section", "dp"),
        ),
        out_specs=P("section", "dp", "tensor"),
        check_vma=False,
    )
```

profile of v0, /device:TPU:32, one launch (start us, length us, event | category | flops | bytes accessed | tf_op | source)
XLA Modules:
  0.0 323.3 jit_solution(6582247643093201020)
XLA Ops:
  6.5 0.8 fusion.10
  7.4 5.0 %sort.73 = (s32[2048]{0:T(1024)}, s32[2048]{0:T(1024)S(1)}) sort(s32[2048]{0:T(1024)S(1)} %fusion.10, s32[2048]{0:T(1024)S(1)} %iota.22), dimensions={0}, to_apply=%region_0.1 | sort | flops 22528 | bytes 32768 | tf_op jit(solution)/shard_map/jit(argsort)/sort | solution.py:25
  12.4 11.8 %gather_fusion = s32[2048]{0:T(1024)S(1)} fusion(s32[2048]{0:T(1024)S(1)} %bitcast.25, s32[2048]{0:T(1024)S(1)} %fusion.19), kind=kCustom, calls=%fused_computation | custom fusion | bytes 24576 | tf_op jit(solution)/shard_map/gather | solution.py:26
  24.2 0.7 all_to_all.12
  24.9 11.4 %all-to-all-start = ((s32[32,1,64]{2,1,0:T(1,128)}), s32[32,1,64]{2,1,0:T(1,128)S(1)}, u32[]{:S(2)}, u32[]{:S(2)}) async-start(s32[32,1,64]{2,1,0:T(1,128)} %all_to_all.12), calls=%async_computation | async-start | bytes 32768 | tf_op jit(solution)/shard_map/all_to_all | solution.py:27
  36.3 8.5 %all-to-all-done = s32[32,1,64]{2,1,0:T(1,128)S(1)} async-done(((s32[32,1,64]{2,1,0:T(1,128)}), s32[32,1,64]{2,1,0:T(1,128)S(1)}, u32[]{:S(2)}, u32[]{:S(2)}) %all-to-all-start) | async-done | bytes 8224 | tf_op jit(solution)/shard_map/all_to_all | solution.py:27
  44.8 13.6 %gather_fusion.1 = bf16[2048,1024]{1,0:T(8,128)(2,1)} fusion(bf16[2008,1024]{1,0:T(8,128)(2,1)} %param.6, s32[2048]{0:T(1024)S(1)} %broadcast_clamp_fusion), kind=kCustom, calls=%fused_computation.1 | custom fusion | bytes 8396800 | tf_op jit(solution)/shard_map/gather | solution.py:31
  58.5 6.1 %all-to-all-start.1 = ((bf16[32,64,1024]{2,1,0:T(8,128)(2,1)}), bf16[32,64,1024]{2,1,0:T(8,128)(2,1)}, u32[]{:S(2)}, u32[]{:S(2)}) async-start(bf16[32,64,1024]{2,1,0:T(8,128)(2,1)} %bitcast.26), calls=%async_computation.1 | async-start | bytes 8388608 | tf_op jit(solution)/shard_map/all_to_all | solution.py:32
  64.6 5.0 %sort.74 = (s32[2048]{0:T(1024)}, s32[2048]{0:T(1024)S(1)}) sort(s32[2048]{0:T(1024)S(1)} %get-tuple-element.10, s32[2048]{0:T(1024)S(1)} %iota.23), dimensions={0}, to_apply=%region_1.2 | sort | flops 22528 | bytes 32768 | tf_op jit(solution)/shard_map/jit(argsort)/sort | solution.py:35
  69.7 5.0 %sort.75 = (s32[2048]{0:T(1024)}, s32[2048]{0:T(1024)S(1)}) sort(s32[2048]{0:T(1024)S(1)} %fusion.13, s32[2048]{0:T(1024)S(1)} %iota.25), dimensions={0}, to_apply=%region_2.3 | sort | flops 22528 | bytes 32768 | tf_op jit(solution)/shard_map/jit(argsort)/sort | solution.py:45
  74.9 84.0 %all-to-all-done.1 = bf16[32,64,1024]{2,1,0:T(8,128)(2,1)} async-done(((bf16[32,64,1024]{2,1,0:T(8,128)(2,1)}), bf16[32,64,1024]{2,1,0:T(8,128)(2,1)}, u32[]{:S(2)}, u32[]{:S(2)}) %all-to-all-start.1) | async-done | bytes 4194336 | tf_op jit(solution)/shard_map/all_to_all | solution.py:32
  159.0 13.7 %gather_fusion.2 = bf16[2048,1024]{1,0:T(8,128)(2,1)} fusion(bf16[2048,1024]{1,0:T(8,128)(2,1)} %bitcast.4, s32[2048]{0:T(1024)S(1)} %fusion.20), kind=kCustom, calls=%fused_computation.2 | custom fusion | bytes 8396800 | tf_op jit(solution)/shard_map/gather | solution.py:36
  172.6 7.8 %fusion.5 = f32[2048,512]{1,0:T(8,128)} fusion(bf16[1024,512]{1,0:T(8,128)(2,1)S(1)} %copy-done, bf16[2048,1024]{1,0:T(8,128)(2,1)} %gather_fusion.2, bf16[1,2048,1024]{2,1,0:T(8,128)(2,1)} %param.5, f32[]{:T(128)S(6)} %convert_element_type.24), kind=kOutput, calls=%fused_computation.12 | convolution fusion | flops 2157969408 | bytes 13631492 | tf_op jit(solution)/shard_map/dot_general | solution.py:51
  180.4 11.7 %gather_fusion.3 = f32[2048,512]{1,0:T(8,128)} fusion(f32[2048,512]{1,0:T(8,128)} %fusion.5, s32[2048]{0:T(1024)S(1)} %broadcast_clamp_fusion.1), kind=kCustom, calls=%fused_computation.3 | custom fusion | bytes 8396800 | tf_op jit(solution)/shard_map/gather | solution.py:52
  192.1 57.2 %all-reduce.1 = bf16[2048,512]{1,0:T(8,128)(2,1)S(1)} all-reduce(f32[2048,512]{1,0:T(8,128)} %gather_fusion.3), channel_id=1, replica_groups=mesh['section'=2,'dp'=16,'tensor'=8] {'tensor'}, use_global_device_ids=true, to_apply=%region_3.4 | all-reduce | flops 1048576 | bytes 6291456 | tf_op jit(solution)/shard_map/psum | solution.py:54
  249.4 19.1 %all_to_all.19 = bf16[16,16,512]{2,1,0:T(8,128)(2,1)S(1)} all-to-all(bf16[16,16,512]{2,1,0:T(8,128)(2,1)S(1)} %bitcast.27), channel_id=1, replica_groups=mesh['section'=2,'dp'=16,'tensor'=8] {'dp'}, dimensions={0} | all-to-all | bytes 524288 | tf_op jit(solution)/shard_map/all_to_all | solution.py:59
  268.4 0.3 collective-permute-start
  268.7 6.1 %collective-permute-done = bf16[16,16,512]{2,1,0:T(8,128)(2,1)S(1)} collective-permute-done((bf16[16,16,512]{2,1,0:T(8,128)(2,1)S(1)}, bf16[16,16,512]{2,1,0:T(8,128)(2,1)S(1)}, u32[]{:S(2)}, u32[]{:S(2)}) %collective-permute-start) | collective-permute-done | bytes 262176 | tf_op jit(solution)/shard_map/ppermute | solution.py:10
  274.8 0.7 copy-done.2
  275.6 5.0 %sort.76 = (s32[2048]{0:T(1024)}, s32[2048]{0:T(1024)S(1)}) sort(s32[2048]{0:T(1024)S(1)} %bitcast.33, s32[2048]{0:T(1024)S(1)} %iota.26), dimensions={0}, to_apply=%region_4.5 | sort | flops 22528 | bytes 32768 | tf_op jit(solution)/shard_map/jit(argsort)/sort | solution.py:61
  280.6 5.0 %sort.77 = (s32[2048]{0:T(1024)}, s32[2048]{0:T(1024)S(1)}) sort(s32[2048]{0:T(1024)S(1)} %get-tuple-element.13, s32[2048]{0:T(1024)S(1)} %iota.27), dimensions={0}, to_apply=%region_5.6 | sort | flops 22528 | bytes 32768 | tf_op jit(solution)/shard_map/jit(argsort)/sort | solution.py:62
  285.7 14.7 %all-gather.2.cloned.1.call-done = bf16[2048,512]{1,0:T(8,128)(2,1)} async-done(((bf16[256,512]{1,0:T(8,128)(2,1)}), bf16[2048,512]{1,0:T(8,128)(2,1)}) %all-gather.2.cloned.1.call-update) | async-done | bytes 2097168 | tf_op jit(solution)/shard_map/all_gather | solution.py:68
  300.4 9.4 %gather_fusion.4 = bf16[2048,512]{1,0:T(8,128)(2,1)S(1)} fusion(bf16[2048,512]{1,0:T(8,128)(2,1)} %all-gather.2.cloned.1.call-done, s32[2048]{0:T(1024)S(1)} %fusion.21), kind=kCustom, calls=%fused_computation.4 | custom fusion | bytes 4202496 | tf_op jit(solution)/shard_map/gather | solution.py:71
  309.8 6.6 %fusion.4 = bf16[1,2048,1024]{2,1,0:T(8,128)(2,1)} fusion(bf16[2048,1024]{1,0:T(8,128)(2,1)} %gather_fusion.2, f32[]{:T(128)S(6)} %sub.48, bf16[2048,512]{1,0:T(8,128)(2,1)S(1)} %gather_fusion.4, bf16[1024,512]{1,0:T(8,128)(2,1)S(1)} %copy-done), kind=kOutput, calls=%fused_computation.11 | convolution fusion | flops 2155872256 | bytes 11534340 | tf_op jit(solution)/shard_map/dot_general | solution.py:72
  (28 shorter events, 0.4 us)
Async XLA Ops:
  6.5 166.1 %copy-start = (bf16[1024,512]{1,0:T(8,128)(2,1)S(1)}, bf16[1024,512]{1,0:T(8,128)(2,1)}, u32[]{:S(2)}) copy-start(bf16[1024,512]{1,0:T(8,128)(2,1)} %param.7) | copy-start | bytes 3145732
  6.5 5.9 %copy-start.1 = (s32[1,2048]{1,0:T(1,128)S(1)}, s32[1,2048]{1,0:T(1,128)}, u32[]{:S(2)}) copy-start(s32[1,2048]{1,0:T(1,128)} %param.8) | copy-start | bytes 24580
  24.9 19.9 %all-to-all-start = ((s32[32,1,64]{2,1,0:T(1,128)}), s32[32,1,64]{2,1,0:T(1,128)S(1)}, u32[]{:S(2)}, u32[]{:S(2)}) async-start(s32[32,1,64]{2,1,0:T(1,128)} %all_to_all.12), calls=%async_computation | async-start | bytes 32768 | tf_op jit(solution)/shard_map/all_to_all | solution.py:27
  58.5 11.2 %copy-start.3 = (s32[1,2048]{1,0:T(1,128)S(1)}, s32[1,2048]{1,0:T(1,128)}, u32[]{:S(2)}) copy-start(s32[1,2048]{1,0:T(1,128)} %param.9) | copy-start | bytes 24580
  58.5 100.5 %all-to-all-start.1 = ((bf16[32,64,1024]{2,1,0:T(8,128)(2,1)}), bf16[32,64,1024]{2,1,0:T(8,128)(2,1)}, u32[]{:S(2)}, u32[]{:S(2)}) async-start(bf16[32,64,1024]{2,1,0:T(8,128)(2,1)} %bitcast.26), calls=%async_computation.1 | async-start | bytes 8388608 | tf_op jit(solution)/shard_map/all_to_all | solution.py:32
  64.5 235.8 %all-gather.2.cloned.1.call-start = ((), (), s32[]{:S(2)}) async-start(), calls=%async_computation.3 | async-start | bytes 2359296 | tf_op jit(solution)/shard_map/all_gather | solution.py:68
  268.4 6.4 %collective-permute-start = (bf16[16,16,512]{2,1,0:T(8,128)(2,1)S(1)}, bf16[16,16,512]{2,1,0:T(8,128)(2,1)S(1)}, u32[]{:S(2)}, u32[]{:S(2)}) collective-permute-start(bf16[16,16,512]{2,1,0:T(8,128)(2,1)S(1)} %all_to_all.19), channel_id=1, source_target_pairs={{0,128},{128,0},{1,129},{129,1},{2,130},{130,2},{3,131},{131,3},{4... | collective-permute-start | bytes 786440 | tf_op jit(solution)/shard_map/ppermute | solution.py:10
  274.8 0.7 copy-start.2
Sparse Core Ops, SparseCore 0:
  275.7 24.6 all-gather.1
where the time goes:
time: 325 us; the launch traced here: 323 us
  waiting for transfers between devices  113 us (35%)
  blocking collectives  76.3 us (23%)
  local copies, waits for them, and re-layouts  62 us (19%)
  other arithmetic  26.1 us (8%)
  starting transfers between devices  17.8 us (5%)
  matrix products  14.4 us (4%)
  between operations  13.5 us (4%)
    all_to_all x1, waiting for transfers between devices, on_device(): lax.all_to_all(looked_up, ('section', 'dp'), split_axis=0, concat_axis=0,...  84 us
    psum x1, blocking collectives, on_device(): summed = lax.psum(ordered_coef, 'tensor')  57.2 us
    all_to_all x1, blocking collectives, on_device(): lax.all_to_all(coef_rows, 'dp', split_axis=0, concat_axis=0, tiled=True)  19.1 us
    all_gather x1, waiting for transfers between devices, on_device(): lax.all_gather(moved_rows.reshape(dp_count * piece_count, -1), 'tensor',...  14.7 us
    gather x1, local copies, waits for them, and re-layouts, on_device(): embed_rows = returned_rows.reshape(tok_count, -1)[undo_order]  13.7 us
    gather x1, local copies, waits for them, and re-layouts, on_device(): looked_up = embedding[local_index]  13.6 us
    gather x1, local copies, waits for them, and re-layouts, on_device(): asked_ids = own_ids[ask_order].reshape(owner_count, per_owner)  11.8 us
    gather x1, local copies, waits for them, and re-layouts, on_device(): ordered_coef = partial_coef[send_order]  11.7 us
  transfers between devices with their start and end apart: 4, of which 4 were waited for; matrix products, arithmetic and copies ran while one was open for 6% of the time, Pallas kernels for 0%

commit v1 on v0

v1 whole, which is shorter than its diff:
```python
import jax
import jax.numpy as jnp
from jax import lax
from jax.experimental import pallas as pl
from jax.experimental.pallas import tpu as pltpu
from jax.sharding import PartitionSpec as P

BF16, F32, I32 = jnp.bfloat16, jnp.float32, jnp.int32
TOK = 2048
FEAT = 1024
RANK = 512
VBLOCK = 2008
LANES = 128
HALF = 1024
VWHOLE = 1920
EARLY = 12


def kernel(acts_hbm, emb_hbm, basis_hbm, ids_ref, route_ref, out_hbm,
           acts, emb, emb_tail, basis, looked, arrived, total, place_e,
           keys, key_col, rank_col, recv_col, send_row, ask, ask_in, ask_col,
           part, core_in, x_in, epart, ecore_in, ex_in,
           slots, coef_in, ebs, eb_in, gathered, coefs,
           load_sem, ask_s, ask_r, emb_s, emb_r, core_s, core_r, x_s, x_r,
           ecore_s, ecore_r, ex_s, ex_r, coef_s, coef_r, eb_s, eb_r,
           ag_s, ag_r, fwd_s, fwd_r, out_s):
    s = lax.axis_index("section")
    d = lax.axis_index("dp")
    t = lax.axis_index("tensor")
    y, zh, x, c = d // 4, d % 4, t // 2, t % 2

    def dev(s_, d_, t_):
        return {"section": s_, "dp": d_, "tensor": t_}

    def remote(src, dst, send_sem, recv_sem, to):
        return pltpu.make_async_remote_copy(
            src, dst, send_sem, recv_sem, device_id=to, device_id_type=pl.DeviceIdType.MESH)

    partner = dev(s, d, x * 2 + 1 - c)

    def dest(k):
        return (y + ((k % 4) + 2)) % 4 * 4 + (zh + ((k // 4) + 2)) % 4

    def source(k):
        return (y + 6 - (k % 4)) % 4 * 4 + (zh + 6 - (k // 4)) % 4

    def loop(n, body, start=0):
        def step(i, carry):
            body(i)
            return carry
        lax.fori_loop(start, n, step, 0)

    lane = lax.broadcasted_iota(I32, (LANES, LANES), 1)
    sub = lax.broadcasted_iota(I32, (LANES, LANES), 0)

    load_basis = pltpu.make_async_copy(basis_hbm, basis, load_sem.at[0])
    load_acts = pltpu.make_async_copy(acts_hbm, acts, load_sem.at[1])
    load_emb = pltpu.make_async_copy(emb_hbm, emb, load_sem.at[2])
    load_basis.start()
    load_acts.start()
    load_emb.start()

    barrier = pltpu.get_barrier_semaphore()

    def greet(to):
        pl.semaphore_signal(barrier, inc=1, device_id=to, device_id_type=pl.DeviceIdType.MESH)

    greet(partner)
    loop(4, lambda j: greet(dev(s, d, (x + j) % 4 * 2 + c)), 1)
    loop(16, lambda i: greet(dev(1 - s, (d + i) % 16, t)))

    @pl.when(s == 1)
    def _():
        loop(16, lambda i: greet(dev(s, (d + i) % 16, t)), 1)

    def column(row):
        return jnp.transpose(jnp.broadcast_to(row, (LANES, LANES)))

    def rank_of_columns(dst):
        def block(b):
            own = column(keys[pl.ds(b, 1), :])
            count = jnp.zeros((LANES, LANES), F32)
            for m in range(16):
                count += jnp.where(keys[m:m + 1, :] < own, 1.0, 0.0)
            rank = jnp.sum(count, axis=1, keepdims=True).astype(I32)
            dst[pl.ds(b * LANES, LANES), :] = jnp.broadcast_to(rank, (LANES, LANES))
        loop(16, block)

    pos16 = (lax.broadcasted_iota(I32, (16, LANES), 0) * LANES
             + lax.broadcasted_iota(I32, (16, LANES), 1))

    @pl.when(s == 1)
    def _():
        keys[...] = ids_ref[...] * TOK + pos16
        rank_of_columns(rank_col)

        def id_column(b):
            key_col[pl.ds(b * LANES, LANES), :] = column(ids_ref[pl.ds(b, 1), :])
        loop(16, id_column)

        def request(m):
            found = jnp.zeros((LANES, LANES), I32)
            for b in range(16):
                rows = slice(b * LANES, (b + 1) * LANES)
                found += jnp.where(rank_col[rows, :] == lane + m * LANES, key_col[rows, :], 0)
            ids = jnp.sum(found.astype(F32), axis=0, keepdims=True).astype(I32)
            ask[m] = jnp.broadcast_to(ids, (8, LANES))
        loop(16, request)

    load_basis.wait()
    load_acts.wait()

    def pack(top, bottom, dst, rows):
        n = top.shape[0]
        left = lax.broadcasted_iota(I32, (n, LANES), 1) < 64
        for g in range(4):
            cols = slice(g * LANES, (g + 1) * LANES)
            a, b = top[:, cols], bottom[:, cols]
            dst[0, g, rows, :] = jnp.where(left, a, pltpu.roll(b, 64, 1))
            dst[1, g, rows, :] = jnp.where(left, pltpu.roll(a, 64, 1), b)

    def project(i):
        top = jnp.dot(acts[pl.ds(i * 256, 256), :], basis[...], preferred_element_type=F32)
        bottom = jnp.dot(acts[pl.ds(HALF + i * 256, 256), :], basis[...], preferred_element_type=F32)
        pack(top, bottom, part, pl.ds(i * 256, 256))
    loop(4, project)

    pl.semaphore_wait(barrier, 4 + 16 + 15 * s)

    def ask_owner(i):
        k, so = i // 2, i % 2
        od = source(k)
        src, dst = ask.at[so * 8 + od // 2], ask_in.at[k]

        @pl.when((so == 1) & (od == d))
        def _():
            pltpu.make_async_copy(src, dst, ask_r.at[k]).start()

        @pl.when((so != 1) | (od != d))
        def _():
            remote(src, dst, ask_s.at[i], ask_r.at[k], dev(so, od, t)).start()

    @pl.when(s == 1)
    def _():
        loop(32, ask_owner)

    core_copy = remote(part.at[1 - c], core_in, core_s, core_r, partner)
    core_copy.start()

    load_emb.wait()
    emb_tail[...] = jnp.zeros_like(emb_tail)
    emb_tail[0:VBLOCK - VWHOLE, :] = emb[VWHOLE:VBLOCK, :]
    first_id = (s * 16 + d) * VBLOCK

    def emb_copy(k):
        return remote(looked.at[pl.ds(k * 64, 64)], arrived.at[pl.ds((2 * k + s) * 64, 64)],
                      emb_s.at[k], emb_r.at[2 * k + s], dev(1, dest(k), t))

    def is_self(k):
        return (s == 1) & (dest(k) == d)

    def send_rows(k):
        @pl.when(is_self(k))
        def _():
            pltpu.make_async_copy(looked.at[pl.ds(k * 64, 64)], arrived.at[pl.ds((2 * k + s) * 64, 64)],
                                  emb_r.at[2 * k + s]).start()

        @pl.when(jnp.logical_not(is_self(k)))
        def _():
            emb_copy(k).start()

    def look_up(i):
        for q in range(2):
            k = 2 * i + q
            pltpu.make_async_copy(ask_in.at[k], ask_in.at[k], ask_r.at[k]).wait()
            ask_col[...] = column(ask_in[k, 0:1, :])
            key_col[q * 64:(q + 1) * 64, :] = ask_col[pl.ds((d % 2) * 64, 64), :] - first_id
        want = key_col[0:LANES, :]
        hot = jnp.concatenate(
            [jnp.where(want == lane + m * LANES, 1.0, 0.0).astype(BF16) for m in range(16)], axis=1)
        rows = jnp.dot(hot[:, :VWHOLE], emb[0:VWHOLE, :], preferred_element_type=F32)
        rows += jnp.dot(hot[:, VWHOLE:], emb_tail[...], preferred_element_type=F32)
        looked[pl.ds(i * LANES, LANES), :] = rows.astype(BF16)

    def serve(i):
        look_up(i)
        send_rows(2 * i)
        send_rows(2 * i + 1)
    loop(4, serve)

    core_copy.wait()

    def x_copy(j):
        to = (x + j) % 4
        return remote(part.at[c, to], x_in.at[j - 1], x_s.at[j - 1], x_r.at[j - 1], dev(s, d, to * 2 + c))

    def add_core(j):
        to = (x + j) % 4
        part[c, to] = part[c, to] + core_in[to]

        @pl.when(j < 4)
        def _():
            x_copy(j).start()
    loop(5, add_core, 1)

    loop(EARLY // 2, serve, 4)
    loop(8, look_up, EARLY // 2)

    def project_rows(i):
        h = jnp.dot(looked[pl.ds(i * 256, 256), :], basis[...], preferred_element_type=F32)
        h = h.reshape(4, 2, 32, RANK)
        pack(h[:, 0].reshape(LANES, RANK), h[:, 1].reshape(LANES, RANK), epart, pl.ds(i * LANES, LANES))
    loop(4, project_rows)
    ecore_copy = remote(epart.at[1 - c], ecore_in, ecore_s, ecore_r, partner)
    ecore_copy.start()

    keys[...] = route_ref[...] - route_ref[...] % TOK + pos16

    def send_column(b):
        key_col[pl.ds(b * LANES, LANES), :] = column(keys[pl.ds(b, 1), :])
    loop(16, send_column)

    def send_rank(m):
        own = keys[pl.ds(m, 1), :]
        count = jnp.zeros((LANES, LANES), F32)
        for b in range(16):
            count += jnp.where(key_col[b * LANES:(b + 1) * LANES, :] < own, 1.0, 0.0)
        send_row[pl.ds(m, 1), :] = jnp.sum(count, axis=0, keepdims=True).astype(I32)
    loop(16, send_rank)

    ecore_copy.wait()

    def ex_copy(j):
        to = (x + j) % 4
        return remote(epart.at[c, to], ex_in.at[j - 1], ex_s.at[j - 1], ex_r.at[j - 1], dev(s, d, to * 2 + c))

    def add_ecore(j):
        to = (x + j) % 4
        epart[c, to] = epart[c, to] + ecore_in[to]

        @pl.when(j < 4)
        def _():
            ex_copy(j).start()
    loop(5, add_ecore, 1)

    keys[...] = route_ref[...]
    rank_of_columns(recv_col)

    @pl.when(s == 1)
    def _():
        def place(b):
            p = rank_col[pl.ds(b * LANES, LANES), :]
            o = p // 64
            k = ((zh + 4 - o % 4 + 2) % 4) * 4 + (y + 4 - (o // 4) % 4 + 2) % 4
            code = (2 * k + o // 16) * 64 + p % 64
            for m in range(16):
                place_e[pl.ds(b * LANES, LANES), m * LANES:(m + 1) * LANES] = (
                    jnp.where(code == lane + m * LANES, 1.0, 0.0).astype(BF16))
        loop(16, place)

    loop(4, lambda j: x_copy(j).wait(), 1)
    mine = (part[c, x] + x_in[0] + x_in[1] + x_in[2]).astype(BF16).astype(F32)
    half_left = lax.broadcasted_iota(I32, (HALF, LANES), 1) < 64
    unpacked = jnp.concatenate([mine, pltpu.roll(mine, 64, 1)], axis=0).astype(BF16)
    coefs[:, 0:LANES] = unpacked

    def order(b):
        hot = jnp.concatenate(
            [jnp.where(send_row[m:m + 1, :] == sub + b * LANES, 1.0, 0.0).astype(BF16)
             for m in range(16)], axis=1)
        rows = jnp.dot(hot, coefs[:, 0:LANES], preferred_element_type=F32)
        packed = jnp.where(lane[0:64] < 64, rows[0:64], pltpu.roll(rows[64:128], 64, 1))
        slots[pl.ds(b * 64, 64), :] = packed.astype(BF16)
    loop(16, order)

    def coef_copy(i):
        to = (d + i) % 16
        return remote(slots.at[pl.ds(to * 64, 64)], coef_in.at[pl.ds(d * 64, 64)],
                      coef_s.at[i], coef_r.at[i], dev(1 - s, to, t))
    loop(16, lambda i: coef_copy(i).start())

    loop(16, send_rows, EARLY)

    loop(4, lambda j: ex_copy(j).wait(), 1)
    ebs[...] = (epart[c, x] + ex_in[0] + ex_in[1] + ex_in[2]).astype(BF16)

    def eb_copy(k):
        return remote(ebs.at[pl.ds(k * 32, 32)], eb_in.at[pl.ds((2 * k + s) * 32, 32)],
                      eb_s.at[k], eb_r.at[2 * k + s], dev(1, dest(k), t))

    def send_eb(k):
        @pl.when(is_self(k))
        def _():
            pltpu.make_async_copy(ebs.at[pl.ds(k * 32, 32)], eb_in.at[pl.ds((2 * k + s) * 32, 32)],
                                  eb_r.at[2 * k + s]).start()

        @pl.when(jnp.logical_not(is_self(k)))
        def _():
            eb_copy(k).start()
    loop(16, send_eb)

    def coef_arrived(i):
        frm = (d + 16 - i) % 16
        rows = coef_in.at[pl.ds(frm * 64, 64)]
        pltpu.make_async_copy(rows, rows, coef_r.at[i]).wait()
    loop(16, coef_arrived)

    def unpack_in(src, n):
        blocks = src[...].astype(F32)
        other = pltpu.roll(blocks, 64, 1)
        both = jnp.concatenate([blocks.reshape(HALF // n, 1, n, LANES),
                                other.reshape(HALF // n, 1, n, LANES)], axis=1)
        return both.reshape(TOK, LANES).astype(BF16)

    coefs[:, 0:LANES] = unpack_in(coef_in, 64)

    def put(b):
        own = recv_col[pl.ds(b * LANES, LANES), :]
        hot = jnp.concatenate(
            [jnp.where(own == lane + m * LANES, 1.0, 0.0).astype(BF16) for m in range(16)], axis=1)
        x_in[b // 8, pl.ds((b % 8) * LANES, LANES), :] = jnp.dot(
            hot, coefs[:, 0:LANES], preferred_element_type=F32)
    loop(16, put)

    @pl.when(s == 1)
    def _():
        def eb_arrived(i):
            rows = eb_in.at[pl.ds(i * 32, 32)]
            pltpu.make_async_copy(rows, rows, eb_r.at[i]).wait()
        loop(32, eb_arrived)
        coefs[:, 0:LANES] = unpack_in(eb_in, 32)

        def take(b):
            rows = pl.ds((b % 8) * LANES, LANES)
            x_in[b // 8, rows, :] = x_in[b // 8, rows, :] - jnp.dot(
                place_e[pl.ds(b * LANES, LANES), :], coefs[:, 0:LANES], preferred_element_type=F32)
        loop(16, take)

    gathered[x, c] = jnp.where(half_left, x_in[0], pltpu.roll(x_in[1], 64, 1)).astype(BF16)

    def ag_copy(j):
        return remote(gathered.at[x, c], gathered.at[x, c], ag_s.at[j - 1], ag_r.at[j - 1],
                      dev(s, d, (x + j) % 4 * 2 + c))

    def fwd_copy(j):
        frm = (x + 4 - j) % 4
        return remote(gathered.at[frm, c], gathered.at[frm, c], fwd_s.at[j], fwd_r.at[j], partner)

    loop(4, lambda j: ag_copy(j).start(), 1)
    fwd_copy(0).start()

    def group(g, rows):
        return jnp.dot(place_e[rows, pl.ds(pl.multiple_of(g * 256, 256), 256)],
                       arrived[pl.ds(g * 256, 256), :], preferred_element_type=F32)

    def wait_group(g):
        def one(i):
            rows = arrived.at[pl.ds(i * 64, 64)]
            pltpu.make_async_copy(rows, rows, emb_r.at[i]).wait()
        loop(g * 4 + 4, one, g * 4)

    @pl.when(s == 1)
    def _():
        wait_group(0)

        def first(i):
            rows = pl.ds(i * 256, 256)
            total[rows, :] = group(0, rows)
        loop(8, first)

    @pl.when(s == 0)
    def _():
        def clear(i):
            total[pl.ds(i * 256, 256), :] = jnp.zeros((256, FEAT), F32)
        loop(8, clear)

    def forward(j):
        frm = (x + 4 - j) % 4
        pltpu.make_async_copy(gathered.at[frm, c], gathered.at[frm, c], ag_r.at[j - 1]).wait()
        fwd_copy(j).start()
    loop(4, forward, 1)

    def one_group(g):
        wait_group(g)

        def add(i):
            rows = pl.ds(i * 256, 256)
            total[rows, :] = total[rows, :] + group(g, rows)
        loop(8, add)

    @pl.when(s == 1)
    def _():
        loop(6, one_group, 1)

    def from_partner(j):
        frm = (x + 4 - j) % 4
        pltpu.make_async_copy(gathered.at[frm, 1 - c], gathered.at[frm, 1 - c], fwd_r.at[j]).wait()
    loop(4, from_partner)
    for g in range(4):
        a, b = gathered[g, 0].astype(F32), gathered[g, 1].astype(F32)
        cols = slice(g * LANES, (g + 1) * LANES)
        coefs[0:HALF, cols] = jnp.where(half_left, a, pltpu.roll(b, 64, 1)).astype(BF16)
        coefs[HALF:TOK, cols] = jnp.where(half_left, pltpu.roll(a, 64, 1), b).astype(BF16)

    def lift(i):
        rows = pl.ds(i * 256, 256)
        total[rows, :] = total[rows, :] + lax.dot_general(
            coefs[rows, :], basis[...], (((1,), (1,)), ((), ())), preferred_element_type=F32)
    loop(8, lift)

    @pl.when(s == 1)
    def _():
        loop(8, one_group, 6)

    def out_copy(i):
        rows = pl.ds(i * 256, 256)
        return pltpu.make_async_copy(acts.at[rows], out_hbm.at[rows], out_s.at[i])

    def finish(i):
        rows = pl.ds(i * 256, 256)
        acts[rows, :] = total[rows, :].astype(BF16)
        out_copy(i).start()
    loop(8, finish)

    @pl.when(s == 1)
    def _():
        def asked(i):
            k, so = i // 2, i % 2

            @pl.when((so != 1) | (source(k) != d))
            def _():
                remote(ask.at[0], ask_in.at[0], ask_s.at[i], ask_r.at[0], partner).wait_send()
        loop(32, asked)

    def sent(k):
        coef_copy(k).wait_send()

        @pl.when(jnp.logical_not(is_self(k)))
        def _():
            emb_copy(k).wait_send()
            eb_copy(k).wait_send()
    loop(16, sent)
    loop(4, lambda j: ag_copy(j).wait_send(), 1)
    loop(4, lambda j: fwd_copy(j).wait_send())
    loop(8, lambda i: out_copy(i).wait())


def on_device(outgoing, embedding, shared_basis, token_ids, row_route):
    any_ = pl.BlockSpec(memory_space=pl.ANY)
    vmem = pl.BlockSpec(memory_space=pltpu.VMEM)
    V, D = pltpu.VMEM, pltpu.SemaphoreType.DMA
    scratch = [
        V((TOK, FEAT), BF16), V((VBLOCK, FEAT), BF16), V((LANES, FEAT), BF16), V((FEAT, RANK), BF16),
        V((HALF, FEAT), BF16), V((TOK, FEAT), BF16), V((TOK, FEAT), F32), V((TOK, TOK), BF16),
        V((16, LANES), I32), V((TOK, LANES), I32), V((TOK, LANES), I32), V((TOK, LANES), I32),
        V((16, LANES), I32), V((16, 8, LANES), I32), V((16, 8, LANES), I32), V((LANES, LANES), I32),
        V((2, 4, HALF, LANES), F32), V((4, HALF, LANES), F32), V((3, HALF, LANES), F32),
        V((2, 4, 512, LANES), F32), V((4, 512, LANES), F32), V((3, 512, LANES), F32),
        V((HALF, LANES), BF16), V((HALF, LANES), BF16), V((512, LANES), BF16), V((HALF, LANES), BF16),
        V((4, 2, HALF, LANES), BF16), V((TOK, RANK), BF16),
        D((3,)), D((32,)), D((16,)), D((16,)), D((32,)), D, D, D((3,)), D((3,)),
        D, D, D((3,)), D((3,)), D((16,)), D((16,)), D((16,)), D((32,)),
        D((3,)), D((3,)), D((4,)), D((4,)), D((8,)),
    ]
    out = pl.pallas_call(
        kernel,
        out_shape=jax.ShapeDtypeStruct((TOK, FEAT), BF16),
        in_specs=[any_, any_, any_, vmem, vmem],
        out_specs=any_,
        scratch_shapes=scratch,
        compiler_params=pltpu.CompilerParams(
            collective_id=0, has_side_effects=True, vmem_limit_bytes=62 * 1024 * 1024),
    )(outgoing[0], embedding, shared_basis,
      token_ids.reshape(16, LANES), row_route.reshape(16, LANES))
    return out[None]


def solution(mesh):
    return jax.shard_map(
        on_device,
        mesh=mesh,
        in_specs=(
            P("section", "dp", "tensor"),
            P(("section", "dp"), "tensor"),
            P("tensor", None),
            P("section", "dp"),
            P("section", "dp"),
        ),
        out_specs=P("section", "dp", "tensor"),
        check_vma=False,
    )
```

time: 325 us -> 157 us (0.48)
  Pallas kernels: 0 us -> 152 us
  waiting for transfers between devices: 113 us -> 0 us
  blocking collectives: 76.3 us -> 0 us
  local copies, waits for them, and re-layouts: 62 us -> 4.64 us
  other arithmetic: 26.1 us -> 0 us
  starting transfers between devices: 17.8 us -> 0 us
  matrix products: 14.4 us -> 0 us
  between operations: 13.5 us -> 0.01 us
    pallas_call x0 -> x1, Pallas kernels: none -> 152 us  [on_device(): pl.pallas_call(kernel, out_shape=jax.ShapeDtypeStruct((TOK, FEAT), BF16),...]
    all_to_all x2 -> x0, waiting for transfers between devices: 92.5 us -> none  [the longest x1 84 us: on_device(): lax.all_to_all(looked_up, ('section', 'dp'), split_axis=0, concat_axis=0,...]
    gather x5 -> x0, local copies, waits for them, and re-layouts: 60.2 us -> none  [the longest x1 13.7 us: on_device(): embed_rows = returned_rows.reshape(tok_count, -1)[undo_order]]
    psum x1 -> x0, blocking collectives: 57.2 us -> none  [on_device(): summed = lax.psum(ordered_coef, 'tensor')]
    sort x5 -> x0, other arithmetic: 25.2 us -> none  [the longest x1 5.04 us: on_device(): ask_order = jnp.argsort(owner_of * tok_count + positions)]
    all_to_all x1 -> x0, blocking collectives: 19.1 us -> none  [on_device(): lax.all_to_all(coef_rows, 'dp', split_axis=0, concat_axis=0, tiled=True)]
    all_to_all x2 -> x0, starting transfers between devices: 17.4 us -> none  [the longest x1 11.4 us: on_device(): lax.all_to_all(asked_ids, ('section', 'dp'), split_axis=0, concat_axis=0,...]
    all_gather x1 -> x0, waiting for transfers between devices: 14.7 us -> none  [on_device(): lax.all_gather(moved_rows.reshape(dp_count * piece_count, -1), 'tensor',...]
  transfers between devices with their start and end apart: 4 -> 0, of which waited for: 4 -> 0; matrix products, arithmetic and copies ran while one was open for 6% -> 0% of each run, Pallas kernels for 0% -> 0%
where the time goes in v1:
time: 157 us
  Pallas kernels  152 us (97%)
  local copies, waits for them, and re-layouts  4.64 us (3%)
    pallas_call x1, Pallas kernels, on_device(): pl.pallas_call(kernel, out_shape=jax.ShapeDtypeStruct((TOK, FEAT), BF16),...  152 us
    unnamed x1, local copies, waits for them, and re-layouts  4.64 us

profile of v1, /device:TPU:32, one launch (start us, length us, event | category | flops | bytes accessed | tf_op | source)
XLA Modules:
  0.0 156.9 jit_solution(8848165588984383845)
XLA Ops:
  0.0 152.2 %shard_map.55 = bf16[2048,1024]{1,0:T(8,128)(2,1)} custom-call(bf16[2048,1024]{1,0:T(8,128)(2,1)} %bitcast.5, bf16[2008,1024]{1,0:T(8,128)(2,1)} %emb_hbm.1, bf16[1024,512]{1,0:T(8,128)(2,1)} %basis_hbm.1, s32[16,128]{1,0:T(8,128)} %bitcast.6, s32[16,128]{1,0:T(8,128)} %bitcast.7), custom_call_target="tpu_custom_call" | custom-call | tf_op jit(solution)/shard_map/pallas_call | solution.py:465
  152.3 4.6 %copy.7 = bf16[1,2048,1024]{2,1,0:T(8,128)(2,1)} copy(bf16[1,2048,1024]{2,1,0:T(8,128)(2,1)} %bitcast.4) | data formatting | bytes 8388608

commit v2 on v1

--- a/solution.py
+++ b/solution.py
@@ -13,15 +13,17 @@
 LANES = 128
 HALF = 1024
 VWHOLE = 1920
-EARLY = 12
+EARLY = 8
+NEXT = 12
+VIA = (10, 12)
 
 
 def kernel(acts_hbm, emb_hbm, basis_hbm, ids_ref, route_ref, out_hbm,
            acts, emb, emb_tail, basis, looked, arrived, total, place_e,
-           keys, key_col, rank_col, recv_col, send_row, ask, ask_in, ask_col,
-           part, core_in, x_in, epart, ecore_in, ex_in,
+           keys, key_col, rank_col, recv_col, send_col, send_row, ask, ask_in, ask_col, relay,
+           part, core_in, x_in, epart, ecore_in, ex_out, ex_in,
            slots, coef_in, ebs, eb_in, gathered, coefs,
-           load_sem, ask_s, ask_r, emb_s, emb_r, core_s, core_r, x_s, x_r,
+           load_sem, ask_s, ask_r, emb_s, emb_r, via_r, via_s, core_s, core_r, x_s, x_r,
            ecore_s, ecore_r, ex_s, ex_r, coef_s, coef_r, eb_s, eb_r,
            ag_s, ag_r, fwd_s, fwd_r, out_s):
     s = lax.axis_index("section")
@@ -38,11 +40,17 @@
 
     partner = dev(s, d, x * 2 + 1 - c)
 
+    def dy(k):
+        return (k // 2) % 4 + 2
+
+    def dz(k):
+        return jnp.where(k < 8, 1 + 2 * (k % 2), 2 - 2 * (k % 2))
+
     def dest(k):
-        return (y + ((k % 4) + 2)) % 4 * 4 + (zh + ((k // 4) + 2)) % 4
+        return (y + dy(k)) % 4 * 4 + (zh + dz(k)) % 4
 
     def source(k):
-        return (y + 6 - (k % 4)) % 4 * 4 + (zh + 6 - (k // 4)) % 4
+        return (y + 8 - dy(k)) % 4 * 4 + (zh + 4 - dz(k)) % 4
 
     def loop(n, body, start=0):
         def step(i, carry):
@@ -107,6 +115,25 @@
             ask[m] = jnp.broadcast_to(ids, (8, LANES))
         loop(16, request)
 
+    pl.semaphore_wait(barrier, 4 + 16 + 15 * s)
+
+    def ask_owner(i):
+        k, so = i // 2, i % 2
+        od = source(k)
+        src, dst = ask.at[so * 8 + od // 2], ask_in.at[k]
+
+        @pl.when((so == 1) & (od == d))
+        def _():
+            pltpu.make_async_copy(src, dst, ask_r.at[k]).start()
+
+        @pl.when((so != 1) | (od != d))
+        def _():
+            remote(src, dst, ask_s.at[i], ask_r.at[k], dev(so, od, t)).start()
+
+    @pl.when(s == 1)
+    def _():
+        loop(32, ask_owner)
+
     load_basis.wait()
     load_acts.wait()
 
@@ -125,25 +152,6 @@
         pack(top, bottom, part, pl.ds(i * 256, 256))
     loop(4, project)
 
-    pl.semaphore_wait(barrier, 4 + 16 + 15 * s)
-
-    def ask_owner(i):
-        k, so = i // 2, i % 2
-        od = source(k)
-        src, dst = ask.at[so * 8 + od // 2], ask_in.at[k]
-
-        @pl.when((so == 1) & (od == d))
-        def _():
-            pltpu.make_async_copy(src, dst, ask_r.at[k]).start()
-
-        @pl.when((so != 1) | (od != d))
-        def _():
-            remote(src, dst, ask_s.at[i], ask_r.at[k], dev(so, od, t)).start()
-
-    @pl.when(s == 1)
-    def _():
-        loop(32, ask_owner)
-
     core_copy = remote(part.at[1 - c], core_in, core_s, core_r, partner)
     core_copy.start()
 
@@ -159,15 +167,28 @@
     def is_self(k):
         return (s == 1) & (dest(k) == d)
 
+    def is_via(k):
+        return (s == 1) & ((k == VIA[0]) | (k == VIA[1]))
+
     def send_rows(k):
         @pl.when(is_self(k))
         def _():
             pltpu.make_async_copy(looked.at[pl.ds(k * 64, 64)], arrived.at[pl.ds((2 * k + s) * 64, 64)],
                                   emb_r.at[2 * k + s]).start()
 
-        @pl.when(jnp.logical_not(is_self(k)))
+        @pl.when(jnp.logical_not(is_self(k) | is_via(k)))
         def _():
             emb_copy(k).start()
+
+    def via_copy(i):
+        k = VIA[i]
+        return remote(looked.at[pl.ds(k * 64, 64)], relay.at[i], emb_s.at[k], via_r.at[i],
+                      dev(1, y * 4 + (zh + 1) % 4, t))
+
+    def hand_on(i):
+        k = VIA[i]
+        return remote(relay.at[i], arrived.at[pl.ds((2 * k + 1) * 64, 64)], via_s.at[i],
+                      emb_r.at[2 * k + 1], dev(1, (y + (k // 2) % 4 + 2) % 4 * 4 + (zh + 1) % 4, t))
 
     def look_up(i):
         for q in range(2):
@@ -186,7 +207,7 @@
         look_up(i)
         send_rows(2 * i)
         send_rows(2 * i + 1)
-    loop(4, serve)
+    loop(2, serve)
 
     core_copy.wait()
 
@@ -203,8 +224,13 @@
             x_copy(j).start()
     loop(5, add_core, 1)
 
-    loop(EARLY // 2, serve, 4)
+    loop(EARLY // 2, serve, 2)
     loop(8, look_up, EARLY // 2)
+
+    @pl.when(s == 1)
+    def _():
+        via_copy(0).start()
+        via_copy(1).start()
 
     def project_rows(i):
         h = jnp.dot(looked[pl.ds(i * 256, 256), :], basis[...], preferred_element_type=F32)
@@ -220,58 +246,91 @@
         key_col[pl.ds(b * LANES, LANES), :] = column(keys[pl.ds(b, 1), :])
     loop(16, send_column)
 
+    def code_of(p):
+        return ((p >> 6) & 1) * HALF + (p >> 7) * 64 + (p & 63)
+
     def send_rank(m):
         own = keys[pl.ds(m, 1), :]
         count = jnp.zeros((LANES, LANES), F32)
         for b in range(16):
             count += jnp.where(key_col[b * LANES:(b + 1) * LANES, :] < own, 1.0, 0.0)
-        send_row[pl.ds(m, 1), :] = jnp.sum(count, axis=0, keepdims=True).astype(I32)
+        send_row[pl.ds(m, 1), :] = code_of(jnp.sum(count, axis=0, keepdims=True).astype(I32))
     loop(16, send_rank)
+
+    def invert(b):
+        found = jnp.zeros((LANES, LANES), I32)
+        for m in range(16):
+            found += jnp.where(send_row[m:m + 1, :] == sub + b * LANES, lane + m * LANES, 0)
+        row = jnp.sum(found.astype(F32), axis=1, keepdims=True).astype(I32)
+        send_col[pl.ds(b * LANES, LANES), :] = jnp.broadcast_to(row, (LANES, LANES))
+    loop(16, invert)
 
     ecore_copy.wait()
 
     def ex_copy(j):
         to = (x + j) % 4
-        return remote(epart.at[c, to], ex_in.at[j - 1], ex_s.at[j - 1], ex_r.at[j - 1], dev(s, d, to * 2 + c))
+        return remote(ex_out.at[j - 1], ex_in.at[j - 1], ex_s.at[j - 1], ex_r.at[j - 1], dev(s, d, to * 2 + c))
 
     def add_ecore(j):
         to = (x + j) % 4
-        epart[c, to] = epart[c, to] + ecore_in[to]
-
-        @pl.when(j < 4)
-        def _():
-            ex_copy(j).start()
-    loop(5, add_ecore, 1)
+        ex_out[j - 1] = (epart[c, to] + ecore_in[to]).astype(BF16)
+        ex_copy(j).start()
+    loop(4, add_ecore, 1)
 
     keys[...] = route_ref[...]
     rank_of_columns(recv_col)
 
+    def recv_code(b):
+        rows = pl.ds(b * LANES, LANES)
+        recv_col[rows, :] = code_of(recv_col[rows, :])
+    loop(16, recv_code)
+
     @pl.when(s == 1)
     def _():
         def place(b):
             p = rank_col[pl.ds(b * LANES, LANES), :]
-            o = p // 64
-            k = ((zh + 4 - o % 4 + 2) % 4) * 4 + (y + 4 - (o // 4) % 4 + 2) % 4
-            code = (2 * k + o // 16) * 64 + p % 64
+            o = p >> 6
+            far = (zh + 4 - (o & 3)) & 3
+            late = 1 - (far & 1)
+            k = late * 8 + ((y + 2 - ((o >> 2) & 3)) & 3) * 2 + ((far >> 1) ^ late)
+            code = (2 * k + (o >> 4)) * 64 + (p & 63)
+            rank_col[pl.ds(b * LANES, LANES), :] = (
+                ((code >> 5) & 1) * HALF + (code >> 6) * 32 + (code & 31))
             for m in range(16):
                 place_e[pl.ds(b * LANES, LANES), m * LANES:(m + 1) * LANES] = (
                     jnp.where(code == lane + m * LANES, 1.0, 0.0).astype(BF16))
         loop(16, place)
 
     loop(4, lambda j: x_copy(j).wait(), 1)
-    mine = (part[c, x] + x_in[0] + x_in[1] + x_in[2]).astype(BF16).astype(F32)
-    half_left = lax.broadcasted_iota(I32, (HALF, LANES), 1) < 64
-    unpacked = jnp.concatenate([mine, pltpu.roll(mine, 64, 1)], axis=0).astype(BF16)
-    coefs[:, 0:LANES] = unpacked
-
-    def order(b):
-        hot = jnp.concatenate(
-            [jnp.where(send_row[m:m + 1, :] == sub + b * LANES, 1.0, 0.0).astype(BF16)
-             for m in range(16)], axis=1)
-        rows = jnp.dot(hot, coefs[:, 0:LANES], preferred_element_type=F32)
-        packed = jnp.where(lane[0:64] < 64, rows[0:64], pltpu.roll(rows[64:128], 64, 1))
-        slots[pl.ds(b * 64, 64), :] = packed.astype(BF16)
-    loop(16, order)
+    mine = (part[c, x] + x_in[0] + x_in[1] + x_in[2]).astype(BF16)
+    gathered[x, c] = mine
+    left = lax.broadcasted_iota(I32, (256, LANES), 1) < 64
+    lanes256 = lax.broadcasted_iota(I32, (512, LANES), 1)
+
+    def pick(src, places, use):
+        for g in range(4):
+            coefs[0:256, g * LANES:(g + 1) * LANES] = src[g * 256:(g + 1) * 256, :]
+
+        def block(i):
+            v = jnp.concatenate([places[pl.ds(i * 256, 256), :], places[pl.ds(HALF + i * 256, 256), :]], axis=0)
+            low = v & 255
+            hot = jnp.concatenate([jnp.where(low == lanes256 + m * LANES, 1.0, 0.0).astype(BF16)
+                                   for m in range(2)], axis=1)
+            rows = jnp.dot(hot, coefs[0:256, :], preferred_element_type=F32)
+            which = (v >> 8) & 3
+            found = rows[:, 0:LANES]
+            for g in range(1, 4):
+                found = jnp.where(which == g, rows[:, g * LANES:(g + 1) * LANES], found)
+            other = pltpu.roll(found, 64, 1)
+            second = v >= HALF
+            top = jnp.where(second[0:256], other[0:256], found[0:256])
+            bottom = jnp.where(second[256:512], found[256:512], other[256:512])
+            use(pl.ds(i * 256, 256), jnp.where(left, top, bottom))
+        loop(4, block)
+
+    def to_slots(rows, value):
+        slots[rows, :] = value.astype(BF16)
+    pick(gathered.at[x, c], send_col, to_slots)
 
     def coef_copy(i):
         to = (d + i) % 16
@@ -279,10 +338,18 @@
                       coef_s.at[i], coef_r.at[i], dev(1 - s, to, t))
     loop(16, lambda i: coef_copy(i).start())
 
-    loop(16, send_rows, EARLY)
+
+    @pl.when(s == 1)
+    def _():
+        for i in range(2):
+            pltpu.make_async_copy(relay.at[i], relay.at[i], via_r.at[i]).wait()
+            hand_on(i).start()
+
+    loop(NEXT, send_rows, EARLY)
 
     loop(4, lambda j: ex_copy(j).wait(), 1)
-    ebs[...] = (epart[c, x] + ex_in[0] + ex_in[1] + ex_in[2]).astype(BF16)
+    ebs[...] = (epart[c, x] + ecore_in[x] + ex_in[0].astype(F32) + ex_in[1].astype(F32)
+                + ex_in[2].astype(F32)).astype(BF16)
 
     def eb_copy(k):
         return remote(ebs.at[pl.ds(k * 32, 32)], eb_in.at[pl.ds((2 * k + s) * 32, 32)],
@@ -298,6 +365,36 @@
         def _():
             eb_copy(k).start()
     loop(16, send_eb)
+
+    loop(16, send_rows, NEXT)
+
+    def group(g, rows):
+        return jnp.dot(place_e[rows, pl.ds(pl.multiple_of(g * 512, 512), 512)],
+                       arrived[pl.ds(g * 512, 512), :], preferred_element_type=F32)
+
+    def wait_group(g):
+        def one(i):
+            rows = arrived.at[pl.ds(i * 64, 64)]
+            pltpu.make_async_copy(rows, rows, emb_r.at[i]).wait()
+        loop(g * 8 + 8, one, g * 8)
+
+    def one_group(g):
+        wait_group(g)
+
+        def add(i):
+            rows = pl.ds(i * 512, 512)
+            total[rows, :] = total[rows, :] + group(g, rows)
+        loop(4, add)
+
+    @pl.when(s == 1)
+    def _():
+        wait_group(0)
+
+        def first(i):
+            rows = pl.ds(i * 512, 512)
+            total[rows, :] = group(0, rows)
+        loop(4, first)
+        one_group(1)
 
     def coef_arrived(i):
         frm = (d + 16 - i) % 16
@@ -305,22 +402,9 @@
         pltpu.make_async_copy(rows, rows, coef_r.at[i]).wait()
     loop(16, coef_arrived)
 
-    def unpack_in(src, n):
-        blocks = src[...].astype(F32)
-        other = pltpu.roll(blocks, 64, 1)
-        both = jnp.concatenate([blocks.reshape(HALF // n, 1, n, LANES),
-                                other.reshape(HALF // n, 1, n, LANES)], axis=1)
-        return both.reshape(TOK, LANES).astype(BF16)
-
-    coefs[:, 0:LANES] = unpack_in(coef_in, 64)
-
-    def put(b):
-        own = recv_col[pl.ds(b * LANES, LANES), :]
-        hot = jnp.concatenate(
-            [jnp.where(own == lane + m * LANES, 1.0, 0.0).astype(BF16) for m in range(16)], axis=1)
-        x_in[b // 8, pl.ds((b % 8) * LANES, LANES), :] = jnp.dot(
-            hot, coefs[:, 0:LANES], preferred_element_type=F32)
-    loop(16, put)
+    def put(rows, value):
+        x_in[0, rows, :] = value
+    pick(coef_in, recv_col, put)
 
     @pl.when(s == 1)
     def _():
@@ -328,15 +412,13 @@
             rows = eb_in.at[pl.ds(i * 32, 32)]
             pltpu.make_async_copy(rows, rows, eb_r.at[i]).wait()
         loop(32, eb_arrived)
-        coefs[:, 0:LANES] = unpack_in(eb_in, 32)
-
-        def take(b):
-            rows = pl.ds((b % 8) * LANES, LANES)
-            x_in[b // 8, rows, :] = x_in[b // 8, rows, :] - jnp.dot(
-                place_e[pl.ds(b * LANES, LANES), :], coefs[:, 0:LANES], preferred_element_type=F32)
-        loop(16, take)
-
-    gathered[x, c] = jnp.where(half_left, x_in[0], pltpu.roll(x_in[1], 64, 1)).astype(BF16)
+
+        def take(rows, value):
+            x_in[0, rows, :] = x_in[0, rows, :] - value
+        pick(eb_in, rank_col, take)
+
+    gathered[x, c] = x_in[0].astype(BF16)
+    half_left = lax.broadcasted_iota(I32, (HALF, LANES), 1) < 64
 
     def ag_copy(j):
         return remote(gathered.at[x, c], gathered.at[x, c], ag_s.at[j - 1], ag_r.at[j - 1],
@@ -348,31 +430,6 @@
 
     loop(4, lambda j: ag_copy(j).start(), 1)
     fwd_copy(0).start()
-
-    def group(g, rows):
-        return jnp.dot(place_e[rows, pl.ds(pl.multiple_of(g * 256, 256), 256)],
-                       arrived[pl.ds(g * 256, 256), :], preferred_element_type=F32)
-
-    def wait_group(g):
-        def one(i):
-            rows = arrived.at[pl.ds(i * 64, 64)]
-            pltpu.make_async_copy(rows, rows, emb_r.at[i]).wait()
-        loop(g * 4 + 4, one, g * 4)
-
-    @pl.when(s == 1)
-    def _():
-        wait_group(0)
-
-        def first(i):
-            rows = pl.ds(i * 256, 256)
-            total[rows, :] = group(0, rows)
-        loop(8, first)
-
-    @pl.when(s == 0)
-    def _():
-        def clear(i):
-            total[pl.ds(i * 256, 256), :] = jnp.zeros((256, FEAT), F32)
-        loop(8, clear)
 
     def forward(j):
         frm = (x + 4 - j) % 4
@@ -380,17 +437,9 @@
         fwd_copy(j).start()
     loop(4, forward, 1)
 
-    def one_group(g):
-        wait_group(g)
-
-        def add(i):
-            rows = pl.ds(i * 256, 256)
-            total[rows, :] = total[rows, :] + group(g, rows)
-        loop(8, add)
-
-    @pl.when(s == 1)
-    def _():
-        loop(6, one_group, 1)
+    @pl.when(s == 1)
+    def _():
+        one_group(2)
 
     def from_partner(j):
         frm = (x + 4 - j) % 4
@@ -402,25 +451,35 @@
         coefs[0:HALF, cols] = jnp.where(half_left, a, pltpu.roll(b, 64, 1)).astype(BF16)
         coefs[HALF:TOK, cols] = jnp.where(half_left, pltpu.roll(a, 64, 1), b).astype(BF16)
 
-    def lift(i):
-        rows = pl.ds(i * 256, 256)
-        total[rows, :] = total[rows, :] + lax.dot_general(
+    def lifted(rows):
+        return lax.dot_general(
             coefs[rows, :], basis[...], (((1,), (1,)), ((), ())), preferred_element_type=F32)
-    loop(8, lift)
-
-    @pl.when(s == 1)
-    def _():
-        loop(8, one_group, 6)
 
     def out_copy(i):
-        rows = pl.ds(i * 256, 256)
+        rows = pl.ds(i * 512, 512)
         return pltpu.make_async_copy(acts.at[rows], out_hbm.at[rows], out_s.at[i])
 
-    def finish(i):
-        rows = pl.ds(i * 256, 256)
-        acts[rows, :] = total[rows, :].astype(BF16)
-        out_copy(i).start()
-    loop(8, finish)
+    @pl.when(s == 0)
+    def _():
+        def finish(i):
+            rows = pl.ds(i * 512, 512)
+            acts[rows, :] = lifted(rows).astype(BF16)
+            out_copy(i).start()
+        loop(4, finish)
+
+    @pl.when(s == 1)
+    def _():
+        def lift(i):
+            rows = pl.ds(i * 512, 512)
+            total[rows, :] = total[rows, :] + lifted(rows)
+        loop(4, lift)
+        wait_group(3)
+
+        def finish(i):
+            rows = pl.ds(i * 512, 512)
+            acts[rows, :] = (total[rows, :] + group(3, rows)).astype(BF16)
+            out_copy(i).start()
+        loop(4, finish)
 
     @pl.when(s == 1)
     def _():
@@ -440,9 +499,14 @@
             emb_copy(k).wait_send()
             eb_copy(k).wait_send()
     loop(16, sent)
+
+    @pl.when(s == 1)
+    def _():
+        hand_on(0).wait_send()
+        hand_on(1).wait_send()
     loop(4, lambda j: ag_copy(j).wait_send(), 1)
     loop(4, lambda j: fwd_copy(j).wait_send())
-    loop(8, lambda i: out_copy(i).wait())
+    loop(4, lambda i: out_copy(i).wait())
 
 
 def on_device(outgoing, embedding, shared_basis, token_ids, row_route):
@@ -452,15 +516,16 @@
     scratch = [
         V((TOK, FEAT), BF16), V((VBLOCK, FEAT), BF16), V((LANES, FEAT), BF16), V((FEAT, RANK), BF16),
         V((HALF, FEAT), BF16), V((TOK, FEAT), BF16), V((TOK, FEAT), F32), V((TOK, TOK), BF16),
-        V((16, LANES), I32), V((TOK, LANES), I32), V((TOK, LANES), I32), V((TOK, LANES), I32),
+        V((16, LANES), I32), V((TOK, LANES), I32), V((TOK, LANES), I32), V((TOK, LANES), I32), V((TOK, LANES), I32),
         V((16, LANES), I32), V((16, 8, LANES), I32), V((16, 8, LANES), I32), V((LANES, LANES), I32),
+        V((2, 64, FEAT), BF16),
         V((2, 4, HALF, LANES), F32), V((4, HALF, LANES), F32), V((3, HALF, LANES), F32),
-        V((2, 4, 512, LANES), F32), V((4, 512, LANES), F32), V((3, 512, LANES), F32),
+        V((2, 4, 512, LANES), F32), V((4, 512, LANES), F32), V((3, 512, LANES), BF16), V((3, 512, LANES), BF16),
         V((HALF, LANES), BF16), V((HALF, LANES), BF16), V((512, LANES), BF16), V((HALF, LANES), BF16),
         V((4, 2, HALF, LANES), BF16), V((TOK, RANK), BF16),
-        D((3,)), D((32,)), D((16,)), D((16,)), D((32,)), D, D, D((3,)), D((3,)),
+        D((3,)), D((32,)), D((16,)), D((16,)), D((32,)), D((2,)), D((2,)), D, D, D((3,)), D((3,)),
         D, D, D((3,)), D((3,)), D((16,)), D((16,)), D((16,)), D((32,)),
-        D((3,)), D((3,)), D((4,)), D((4,)), D((8,)),
+        D((3,)), D((3,)), D((4,)), D((4,)), D((4,)),
     ]
     out = pl.pallas_call(
         kernel,

time: 157 us -> 125 us (0.80); the launches traced: 157 us -> 123 us
  Pallas kernels: 152 us -> 118 us
    pallas_call x1, Pallas kernels: 152 us -> 118 us  [on_device(): pl.pallas_call(kernel, out_shape=jax.ShapeDtypeStruct((TOK, FEAT), BF16),...]
where the time goes in v2:
time: 125 us; the launch traced here: 123 us
  Pallas kernels  118 us (94%)
  local copies, waits for them, and re-layouts  4.64 us (4%)
    pallas_call x1, Pallas kernels, on_device(): pl.pallas_call(kernel, out_shape=jax.ShapeDtypeStruct((TOK, FEAT), BF16),...  118 us
    unnamed x1, local copies, waits for them, and re-layouts  4.64 us

profile of v2, /device:TPU:32, one launch (start us, length us, event | category | flops | bytes accessed | tf_op | source)
XLA Modules:
  0.0 122.9 jit_solution(1602315627401204533)
XLA Ops:
  0.0 118.3 %shard_map.55 = bf16[2048,1024]{1,0:T(8,128)(2,1)} custom-call(bf16[2048,1024]{1,0:T(8,128)(2,1)} %bitcast.5, bf16[2008,1024]{1,0:T(8,128)(2,1)} %emb_hbm.1, bf16[1024,512]{1,0:T(8,128)(2,1)} %basis_hbm.1, s32[16,128]{1,0:T(8,128)} %bitcast.6, s32[16,128]{1,0:T(8,128)} %bitcast.7), custom_call_target="tpu_custom_call" | custom-call | tf_op jit(solution)/shard_map/pallas_call | solution.py:530
  118.3 4.6 %copy.7 = bf16[1,2048,1024]{2,1,0:T(8,128)(2,1)} copy(bf16[1,2048,1024]{2,1,0:T(8,128)(2,1)} %bitcast.4) | data formatting | bytes 8388608

commit v3 on v2

--- a/solution.py
+++ b/solution.py
@@ -13,19 +13,18 @@
 LANES = 128
 HALF = 1024
 VWHOLE = 1920
-EARLY = 8
-NEXT = 12
-VIA = (10, 12)
-
-
-def kernel(acts_hbm, emb_hbm, basis_hbm, ids_ref, route_ref, out_hbm,
-           acts, emb, emb_tail, basis, looked, arrived, total, place_e,
+EARLY = 10
+NEXT = 10
+VIA = (0, 2)
+
+
+def kernel(acts_hbm, emb_hbm, basis_hbm, ids_ref, route_ref, acts, emb, emb_tail, basis, looked, arrived, total, place_e,
            keys, key_col, rank_col, recv_col, send_col, send_row, ask, ask_in, ask_col, relay,
            part, core_in, x_in, epart, ecore_in, ex_out, ex_in,
            slots, coef_in, ebs, eb_in, gathered, coefs,
            load_sem, ask_s, ask_r, emb_s, emb_r, via_r, via_s, core_s, core_r, x_s, x_r,
            ecore_s, ecore_r, ex_s, ex_r, coef_s, coef_r, eb_s, eb_r,
-           ag_s, ag_r, fwd_s, fwd_r, out_s):
+           ag_s, ag_r, fwd_s, fwd_r):
     s = lax.axis_index("section")
     d = lax.axis_index("dp")
     t = lax.axis_index("tensor")
@@ -40,17 +39,20 @@
 
     partner = dev(s, d, x * 2 + 1 - c)
 
+    def near(k):
+        return (k >= 4) & (k < 12)
+
     def dy(k):
-        return (k // 2) % 4 + 2
+        return jnp.where(near(k), (k + 12) // 2, jnp.where(k < 4, k + 6, k + 14) // 2) % 4
 
     def dz(k):
-        return jnp.where(k < 8, 1 + 2 * (k % 2), 2 - 2 * (k % 2))
+        return jnp.where(near(k), 1 + 2 * (k % 2), 2 - 2 * (k % 2))
 
     def dest(k):
         return (y + dy(k)) % 4 * 4 + (zh + dz(k)) % 4
 
     def source(k):
-        return (y + 8 - dy(k)) % 4 * 4 + (zh + 4 - dz(k)) % 4
+        return (y + 4 - dy(k)) % 4 * 4 + (zh + 4 - dz(k)) % 4
 
     def loop(n, body, start=0):
         def step(i, carry):
@@ -180,15 +182,19 @@
         def _():
             emb_copy(k).start()
 
+        @pl.when(is_via(k))
+        def _():
+            via_copy(k // 2).start()
+
     def via_copy(i):
-        k = VIA[i]
+        k = 2 * i
         return remote(looked.at[pl.ds(k * 64, 64)], relay.at[i], emb_s.at[k], via_r.at[i],
                       dev(1, y * 4 + (zh + 1) % 4, t))
 
     def hand_on(i):
         k = VIA[i]
         return remote(relay.at[i], arrived.at[pl.ds((2 * k + 1) * 64, 64)], via_s.at[i],
-                      emb_r.at[2 * k + 1], dev(1, (y + (k // 2) % 4 + 2) % 4 * 4 + (zh + 1) % 4, t))
+                      emb_r.at[2 * k + 1], dev(1, (y + dy(k)) % 4 * 4 + (zh + 1) % 4, t))
 
     def look_up(i):
         for q in range(2):
@@ -227,11 +233,6 @@
     loop(EARLY // 2, serve, 2)
     loop(8, look_up, EARLY // 2)
 
-    @pl.when(s == 1)
-    def _():
-        via_copy(0).start()
-        via_copy(1).start()
-
     def project_rows(i):
         h = jnp.dot(looked[pl.ds(i * 256, 256), :], basis[...], preferred_element_type=F32)
         h = h.reshape(4, 2, 32, RANK)
@@ -240,6 +241,12 @@
     ecore_copy = remote(epart.at[1 - c], ecore_in, ecore_s, ecore_r, partner)
     ecore_copy.start()
 
+    @pl.when(s == 1)
+    def _():
+        for i in range(2):
+            pltpu.make_async_copy(relay.at[i], relay.at[i], via_r.at[i]).wait()
+            hand_on(i).start()
+
     keys[...] = route_ref[...] - route_ref[...] % TOK + pos16
 
     def send_column(b):
@@ -290,9 +297,10 @@
         def place(b):
             p = rank_col[pl.ds(b * LANES, LANES), :]
             o = p >> 6
-            far = (zh + 4 - (o & 3)) & 3
-            late = 1 - (far & 1)
-            k = late * 8 + ((y + 2 - ((o >> 2) & 3)) & 3) * 2 + ((far >> 1) ^ late)
+            to_y, to_z = (y + 4 - ((o >> 2) & 3)) & 3, (zh + 4 - (o & 3)) & 3
+            odd = to_z & 1
+            e = ((to_y + 1) & 3) * 2 + 1 - (to_z >> 1)
+            k = jnp.where(odd == 1, 4 + to_y * 2 + (to_z >> 1), e + 8 * (e >> 2))
             code = (2 * k + (o >> 4)) * 64 + (p & 63)
             rank_col[pl.ds(b * LANES, LANES), :] = (
                 ((code >> 5) & 1) * HALF + (code >> 6) * 32 + (code & 31))
@@ -339,12 +347,6 @@
     loop(16, lambda i: coef_copy(i).start())
 
 
-    @pl.when(s == 1)
-    def _():
-        for i in range(2):
-            pltpu.make_async_copy(relay.at[i], relay.at[i], via_r.at[i]).wait()
-            hand_on(i).start()
-
     loop(NEXT, send_rows, EARLY)
 
     loop(4, lambda j: ex_copy(j).wait(), 1)
@@ -455,16 +457,11 @@
         return lax.dot_general(
             coefs[rows, :], basis[...], (((1,), (1,)), ((), ())), preferred_element_type=F32)
 
-    def out_copy(i):
-        rows = pl.ds(i * 512, 512)
-        return pltpu.make_async_copy(acts.at[rows], out_hbm.at[rows], out_s.at[i])
-
     @pl.when(s == 0)
     def _():
         def finish(i):
             rows = pl.ds(i * 512, 512)
             acts[rows, :] = lifted(rows).astype(BF16)
-            out_copy(i).start()
         loop(4, finish)
 
     @pl.when(s == 1)
@@ -478,7 +475,6 @@
         def finish(i):
             rows = pl.ds(i * 512, 512)
             acts[rows, :] = (total[rows, :] + group(3, rows)).astype(BF16)
-            out_copy(i).start()
         loop(4, finish)
 
     @pl.when(s == 1)
@@ -506,7 +502,6 @@
         hand_on(1).wait_send()
     loop(4, lambda j: ag_copy(j).wait_send(), 1)
     loop(4, lambda j: fwd_copy(j).wait_send())
-    loop(4, lambda i: out_copy(i).wait())
 
 
 def on_device(outgoing, embedding, shared_basis, token_ids, row_route):
@@ -514,7 +509,7 @@
     vmem = pl.BlockSpec(memory_space=pltpu.VMEM)
     V, D = pltpu.VMEM, pltpu.SemaphoreType.DMA
     scratch = [
-        V((TOK, FEAT), BF16), V((VBLOCK, FEAT), BF16), V((LANES, FEAT), BF16), V((FEAT, RANK), BF16),
+        V((VBLOCK, FEAT), BF16), V((LANES, FEAT), BF16), V((FEAT, RANK), BF16),
         V((HALF, FEAT), BF16), V((TOK, FEAT), BF16), V((TOK, FEAT), F32), V((TOK, TOK), BF16),
         V((16, LANES), I32), V((TOK, LANES), I32), V((TOK, LANES), I32), V((TOK, LANES), I32), V((TOK, LANES), I32),
         V((16, LANES), I32), V((16, 8, LANES), I32), V((16, 8, LANES), I32), V((LANES, LANES), I32),
@@ -525,16 +520,16 @@
         V((4, 2, HALF, LANES), BF16), V((TOK, RANK), BF16),
         D((3,)), D((32,)), D((16,)), D((16,)), D((32,)), D((2,)), D((2,)), D, D, D((3,)), D((3,)),
         D, D, D((3,)), D((3,)), D((16,)), D((16,)), D((16,)), D((32,)),
-        D((3,)), D((3,)), D((4,)), D((4,)), D((4,)),
+        D((3,)), D((3,)), D((4,)), D((4,)),
     ]
     out = pl.pallas_call(
         kernel,
-        out_shape=jax.ShapeDtypeStruct((TOK, FEAT), BF16),
+        out_shape=pltpu.VMEM((TOK, FEAT), BF16),
         in_specs=[any_, any_, any_, vmem, vmem],
-        out_specs=any_,
+        out_specs=vmem,
         scratch_shapes=scratch,
         compiler_params=pltpu.CompilerParams(
-            collective_id=0, has_side_effects=True, vmem_limit_bytes=62 * 1024 * 1024),
+            collective_id=0, has_side_effects=True, vmem_limit_bytes=57 * 1024 * 1024),
     )(outgoing[0], embedding, shared_basis,
       token_ids.reshape(16, LANES), row_route.reshape(16, LANES))
     return out[None]

time: 125 us -> 108 us (0.86)
  Pallas kernels: 118 us -> 104 us
  local copies, waits for them, and re-layouts: 4.64 us -> 2.02 us
    pallas_call x1, Pallas kernels: 118 us -> 104 us  [on_device(): pl.pallas_call(kernel, out_shape=pltpu.VMEM((TOK, FEAT), BF16), in_specs=...]
    unnamed x1, local copies, waits for them, and re-layouts: 4.64 us -> 2.02 us
where the time goes in v3:
time: 108 us; the launch traced here: 107 us
  Pallas kernels  104 us (96%)
  local copies, waits for them, and re-layouts  2.02 us (2%)
    pallas_call x1, Pallas kernels, on_device(): pl.pallas_call(kernel, out_shape=pltpu.VMEM((TOK, FEAT), BF16), in_specs=...  104 us

profile of v3, /device:TPU:32, one launch (start us, length us, event | category | flops | bytes accessed | tf_op | source)
XLA Modules:
  0.0 106.5 jit_solution(14279617887535281573)
XLA Ops:
  0.0 104.5 %shard_map.55 = bf16[2048,1024]{1,0:T(8,128)(2,1)S(1)} custom-call(bf16[2048,1024]{1,0:T(8,128)(2,1)} %bitcast.5, bf16[2008,1024]{1,0:T(8,128)(2,1)} %emb_hbm.1, bf16[1024,512]{1,0:T(8,128)(2,1)} %basis_hbm.1, s32[16,128]{1,0:T(8,128)} %bitcast.6, s32[16,128]{1,0:T(8,128)} %bitcast.7), custom_call_target="tpu_custom_call" | custom-call | tf_op jit(solution)/shard_map/pallas_call | solution.py:525
  104.5 2.0 %copy.7 = bf16[1,2048,1024]{2,1,0:T(8,128)(2,1)} copy(bf16[1,2048,1024]{2,1,0:T(8,128)(2,1)S(1)} %bitcast.4) | data formatting | bytes 8388608

commit v4 on v3

--- a/solution.py
+++ b/solution.py
@@ -13,14 +13,13 @@
 LANES = 128
 HALF = 1024
 VWHOLE = 1920
-EARLY = 10
-NEXT = 10
+EARLY = 8
 VIA = (0, 2)
 
 
 def kernel(acts_hbm, emb_hbm, basis_hbm, ids_ref, route_ref, acts, emb, emb_tail, basis, looked, arrived, total, place_e,
            keys, key_col, rank_col, recv_col, send_col, send_row, ask, ask_in, ask_col, relay,
-           part, core_in, x_in, epart, ecore_in, ex_out, ex_in,
+           part, core_in, x_out, x_in, epart, ecore_in, ex_out, ex_in,
            slots, coef_in, ebs, eb_in, gathered, coefs,
            load_sem, ask_s, ask_r, emb_s, emb_r, via_r, via_s, core_s, core_r, x_s, x_r,
            ecore_s, ecore_r, ex_s, ex_r, coef_s, coef_r, eb_s, eb_r,
@@ -218,20 +217,19 @@
     core_copy.wait()
 
     def x_copy(j):
-        to = (x + j) % 4
-        return remote(part.at[c, to], x_in.at[j - 1], x_s.at[j - 1], x_r.at[j - 1], dev(s, d, to * 2 + c))
+        return remote(x_out.at[j - 1], x_in.at[j - 1], x_s.at[j - 1], x_r.at[j - 1],
+                      dev(s, d, (x + j) % 4 * 2 + c))
 
     def add_core(j):
         to = (x + j) % 4
-        part[c, to] = part[c, to] + core_in[to]
-
-        @pl.when(j < 4)
-        def _():
-            x_copy(j).start()
-    loop(5, add_core, 1)
+        x_out[j - 1] = (part[c, to] + core_in[to]).astype(BF16)
+        x_copy(j).start()
+    loop(4, add_core, 1)
 
     loop(EARLY // 2, serve, 2)
     loop(8, look_up, EARLY // 2)
+    first_late = EARLY + s
+    loop(first_late, send_rows, EARLY)
 
     def project_rows(i):
         h = jnp.dot(looked[pl.ds(i * 256, 256), :], basis[...], preferred_element_type=F32)
@@ -284,33 +282,9 @@
         ex_copy(j).start()
     loop(4, add_ecore, 1)
 
-    keys[...] = route_ref[...]
-    rank_of_columns(recv_col)
-
-    def recv_code(b):
-        rows = pl.ds(b * LANES, LANES)
-        recv_col[rows, :] = code_of(recv_col[rows, :])
-    loop(16, recv_code)
-
-    @pl.when(s == 1)
-    def _():
-        def place(b):
-            p = rank_col[pl.ds(b * LANES, LANES), :]
-            o = p >> 6
-            to_y, to_z = (y + 4 - ((o >> 2) & 3)) & 3, (zh + 4 - (o & 3)) & 3
-            odd = to_z & 1
-            e = ((to_y + 1) & 3) * 2 + 1 - (to_z >> 1)
-            k = jnp.where(odd == 1, 4 + to_y * 2 + (to_z >> 1), e + 8 * (e >> 2))
-            code = (2 * k + (o >> 4)) * 64 + (p & 63)
-            rank_col[pl.ds(b * LANES, LANES), :] = (
-                ((code >> 5) & 1) * HALF + (code >> 6) * 32 + (code & 31))
-            for m in range(16):
-                place_e[pl.ds(b * LANES, LANES), m * LANES:(m + 1) * LANES] = (
-                    jnp.where(code == lane + m * LANES, 1.0, 0.0).astype(BF16))
-        loop(16, place)
-
     loop(4, lambda j: x_copy(j).wait(), 1)
-    mine = (part[c, x] + x_in[0] + x_in[1] + x_in[2]).astype(BF16)
+    mine = (part[c, x] + core_in[x] + x_in[0].astype(F32) + x_in[1].astype(F32)
+            + x_in[2].astype(F32)).astype(BF16)
     gathered[x, c] = mine
     left = lax.broadcasted_iota(I32, (256, LANES), 1) < 64
     lanes256 = lax.broadcasted_iota(I32, (512, LANES), 1)
@@ -347,8 +321,6 @@
     loop(16, lambda i: coef_copy(i).start())
 
 
-    loop(NEXT, send_rows, EARLY)
-
     loop(4, lambda j: ex_copy(j).wait(), 1)
     ebs[...] = (epart[c, x] + ecore_in[x] + ex_in[0].astype(F32) + ex_in[1].astype(F32)
                 + ex_in[2].astype(F32)).astype(BF16)
@@ -368,7 +340,32 @@
             eb_copy(k).start()
     loop(16, send_eb)
 
-    loop(16, send_rows, NEXT)
+    loop(16, send_rows, first_late)
+
+    keys[...] = route_ref[...]
+    rank_of_columns(recv_col)
+
+    def recv_code(b):
+        rows = pl.ds(b * LANES, LANES)
+        recv_col[rows, :] = code_of(recv_col[rows, :])
+    loop(16, recv_code)
+
+    @pl.when(s == 1)
+    def _():
+        def place(b):
+            p = rank_col[pl.ds(b * LANES, LANES), :]
+            o = p >> 6
+            to_y, to_z = (y + 4 - ((o >> 2) & 3)) & 3, (zh + 4 - (o & 3)) & 3
+            odd = to_z & 1
+            e = ((to_y + 1) & 3) * 2 + 1 - (to_z >> 1)
+            k = jnp.where(odd == 1, 4 + to_y * 2 + (to_z >> 1), e + 8 * (e >> 2))
+            code = (2 * k + (o >> 4)) * 64 + (p & 63)
+            rank_col[pl.ds(b * LANES, LANES), :] = (
+                ((code >> 5) & 1) * HALF + (code >> 6) * 32 + (code & 31))
+            for m in range(16):
+                place_e[pl.ds(b * LANES, LANES), m * LANES:(m + 1) * LANES] = (
+                    jnp.where(code == lane + m * LANES, 1.0, 0.0).astype(BF16))
+        loop(16, place)
 
     def group(g, rows):
         return jnp.dot(place_e[rows, pl.ds(pl.multiple_of(g * 512, 512), 512)],
@@ -396,7 +393,6 @@
             rows = pl.ds(i * 512, 512)
             total[rows, :] = group(0, rows)
         loop(4, first)
-        one_group(1)
 
     def coef_arrived(i):
         frm = (d + 16 - i) % 16
@@ -405,7 +401,7 @@
     loop(16, coef_arrived)
 
     def put(rows, value):
-        x_in[0, rows, :] = value
+        core_in[0, rows, :] = value
     pick(coef_in, recv_col, put)
 
     @pl.when(s == 1)
@@ -416,10 +412,10 @@
         loop(32, eb_arrived)
 
         def take(rows, value):
-            x_in[0, rows, :] = x_in[0, rows, :] - value
+            core_in[0, rows, :] = core_in[0, rows, :] - value
         pick(eb_in, rank_col, take)
 
-    gathered[x, c] = x_in[0].astype(BF16)
+    gathered[x, c] = core_in[0].astype(BF16)
     half_left = lax.broadcasted_iota(I32, (HALF, LANES), 1) < 64
 
     def ag_copy(j):
@@ -432,6 +428,10 @@
 
     loop(4, lambda j: ag_copy(j).start(), 1)
     fwd_copy(0).start()
+
+    @pl.when(s == 1)
+    def _():
+        one_group(1)
 
     def forward(j):
         frm = (x + 4 - j) % 4
@@ -514,7 +514,7 @@
         V((16, LANES), I32), V((TOK, LANES), I32), V((TOK, LANES), I32), V((TOK, LANES), I32), V((TOK, LANES), I32),
         V((16, LANES), I32), V((16, 8, LANES), I32), V((16, 8, LANES), I32), V((LANES, LANES), I32),
         V((2, 64, FEAT), BF16),
-        V((2, 4, HALF, LANES), F32), V((4, HALF, LANES), F32), V((3, HALF, LANES), F32),
+        V((2, 4, HALF, LANES), F32), V((4, HALF, LANES), F32), V((3, HALF, LANES), BF16), V((3, HALF, LANES), BF16),
         V((2, 4, 512, LANES), F32), V((4, 512, LANES), F32), V((3, 512, LANES), BF16), V((3, 512, LANES), BF16),
         V((HALF, LANES), BF16), V((HALF, LANES), BF16), V((512, LANES), BF16), V((HALF, LANES), BF16),
         V((4, 2, HALF, LANES), BF16), V((TOK, RANK), BF16),

time: 108 us -> 104 us (0.963); the launches traced: 107 us -> 104 us
  Pallas kernels: 104 us -> 102 us
    pallas_call x1, Pallas kernels: 104 us -> 102 us  [on_device(): pl.pallas_call(kernel, out_shape=pltpu.VMEM((TOK, FEAT), BF16), in_specs=...]
where the time goes in v4:
time: 104 us
  Pallas kernels  102 us (98%)
  local copies, waits for them, and re-layouts  2.02 us (2%)
    pallas_call x1, Pallas kernels, on_device(): pl.pallas_call(kernel, out_shape=pltpu.VMEM((TOK, FEAT), BF16), in_specs=...  102 us

profile of v4, /device:TPU:32, one launch (start us, length us, event | category | flops | bytes accessed | tf_op | source)
XLA Modules:
  0.0 103.9 jit_solution(9581212010381169136)
XLA Ops:
  0.0 101.9 %shard_map.55 = bf16[2048,1024]{1,0:T(8,128)(2,1)S(1)} custom-call(bf16[2048,1024]{1,0:T(8,128)(2,1)} %bitcast.5, bf16[2008,1024]{1,0:T(8,128)(2,1)} %emb_hbm.1, bf16[1024,512]{1,0:T(8,128)(2,1)} %basis_hbm.1, s32[16,128]{1,0:T(8,128)} %bitcast.6, s32[16,128]{1,0:T(8,128)} %bitcast.7), custom_call_target="tpu_custom_call" | custom-call | tf_op jit(solution)/shard_map/pallas_call | solution.py:525
  101.9 2.0 %copy.7 = bf16[1,2048,1024]{2,1,0:T(8,128)(2,1)} copy(bf16[1,2048,1024]{2,1,0:T(8,128)(2,1)S(1)} %bitcast.4) | data formatting | bytes 8388608
